TPU v7x, 32 devices: a whole 2x2x4 slice. The times are simulated.
32 devices in a mesh: group: 2 (over y), expert: 8 (over z, x), tensor: 2 (over core).
Axes of the slice: x: 2, y: 2, z: 4, core: 2. Of those that a mesh axis runs over, the one named last changes fastest.
Arguments:
- tokens: bfloat16 [1024, 3072], P(('group', 'expert'), 'tensor'), parts along dimension 0, may hold values from -6 to 6
- route_ids: int32 [1024, 4], P(('group', 'expert')), parts along dimension 0, may hold values from 0 to 7, all different within a row; in each aligned block of 64 rows (0 to 63, 64 to 127, ...) at most 64 rows name the same one
- gates: float32 [1024, 4], P(('group', 'expert')), parts along dimension 0, may hold values from 0.1 to 1
- w_up: bfloat16 [8, 3072, 5376], P('expert', None, 'tensor'), may hold values from -0.109375 to 0.109375
- w_down: bfloat16 [8, 5376, 3072], P('expert', 'tensor'), may hold values from -0.109375 to 0.109375
Outputs:
- mixed: bfloat16 [1024, 3072], P(('group', 'expert'), 'tensor'), parts along dimension 0
There are 2 independent parts, one for each index of `group`. A program takes and returns all parts, laid end to end along the dimension named above; an argument that names none is the same for every part. Nothing has to cross between parts.
Inputs may be any that keep to these rules, and one draw needn't show every extreme that they name: `route_ids`: among the 64 rows of one owner, no expert is named by more than 64 routes, and in every draw some expert is named by exactly 64; each row names 4 different experts.
All inputs are finite; a program needn't handle non-finite values.
Results may differ from a plain program's by a relative error of at most 0.0085.
Values may be sent and summed in bfloat16 or wider, within the bound.
A program may use at most 128 MiB of HBM per device.

v0:
```python
import jax
import jax.numpy as jnp
from jax import lax
from jax.sharding import PartitionSpec as P


def body(tokens, route_ids, gates, w_up, w_down):
    experts = lax.axis_size("expert")
    tok_rows = route_ids.shape[0]
    per_token = route_ids.shape[1]
    capacity = min(tok_rows, 2 * tok_rows * per_token // experts)
    slot_count = experts * capacity
    flat_ids = route_ids.reshape(-1)
    onehot = (flat_ids[:, None] == jnp.arange(experts, dtype=jnp.int32)[None, :]).astype(jnp.int32)
    within = jnp.sum((jnp.cumsum(onehot, axis=0) - onehot) * onehot, axis=1)
    target = flat_ids * capacity + within
    up_weight = w_up[0]
    down_weight = w_down[0]
    repeated = jnp.repeat(tokens, per_token, axis=0)
    arrived = lax.all_to_all(
        jnp.zeros((slot_count, tokens.shape[1]), tokens.dtype).at[target].set(repeated),
        "expert",
        split_axis=0,
        concat_axis=0,
        tiled=True,
    )
    upward = jnp.dot(
        lax.all_gather(arrived, "tensor", axis=1, tiled=True),
        up_weight,
        preferred_element_type=jnp.float32,
    )
    hidden = jax.nn.silu(upward).astype(jnp.bfloat16)
    partial_out = jnp.dot(hidden, down_weight, preferred_element_type=jnp.float32)
    results = lax.psum_scatter(
        partial_out.astype(jnp.bfloat16), "tensor", scatter_dimension=1, tiled=True
    ).astype(jnp.float32)
    returned = lax.all_to_all(
        results.astype(jnp.bfloat16), "expert", split_axis=0, concat_axis=0, tiled=True
    ).astype(results.dtype)
    picked = returned[target].reshape(tok_rows, per_token, -1)
    summed = jnp.sum(picked * gates[:, :, None], axis=1)
    return summed.astype(jnp.bfloat16)


def solution(mesh):
    return jax.shard_map(
        body,
        mesh=mesh,
        in_specs=(
            P(("group", "expert"), "tensor"),
            P(("group", "expert"), None),
            P(("group", "expert"), None),
            P("expert", None, "tensor"),
            P("expert", "tensor", None),
        ),
        out_specs=P(("group", "expert"), "tensor"),
        check_vma=False,
    )
```

profile of v0, /device:TPU:0, one launch (start us, length us, event | category | flops | bytes accessed | tf_op | source)
XLA Modules:
  0.0 171.5 jit_solution(7505985693127474529)
XLA Ops:
  6.5 0.0 all-gather.2.cloned.1.call-start
  6.5 0.8 copy.8
  7.3 0.1 eq.29
  7.4 0.1 eq.25
  7.5 0.7 broadcast_multiply_fusion
  8.2 0.6 reduce-window.6
  8.8 0.2 slice_reduce_fusion
  9.0 0.1 copy.7
  9.1 0.1 mul.33
  9.3 1.1 broadcast_in_dim.5
  10.4 0.2 reshape.75
  10.6 0.1 fusion.15
  10.7 2.3 %scatter_custom_fusion = bf16[512,1536]{1,0:T(8,128)(2,1)S(1)} fusion(s32[256]{0:T(256)S(1)} %bitcast.32, bf16[256,1536]{1,0:T(8,128)(2,1)S(1)} %reshape.75, bf16[]{:T(256)} %constant.6.clone.1), kind=kCustom, calls=%fused_computation.11 | custom fusion | bytes 1572866 | tf_op jit(solution)/shard_map/scatter | solution.py:21
  13.0 44.2 %all_to_all.21 = bf16[8,64,1536]{2,1,0:T(8,128)(2,1)} all-to-all(bf16[8,64,1536]{2,1,0:T(8,128)(2,1)S(1)} %bitcast.30), channel_id=1, replica_groups=mesh['group'=2,'expert'=8,'tensor'=2] {'expert'}, dimensions={0} | all-to-all | bytes 3145728 | tf_op jit(solution)/shard_map/all_to_all | solution.py:20
  57.2 0.0 all-gather.2.cloned.1.call-update
  57.2 0.2 reduce-scatter.2.cloned.1.call-start
  57.4 11.1 %all-gather.2.cloned.1.call-done = bf16[512,3072]{1,0:T(8,128)(2,1)} async-done(((bf16[512,1536]{1,0:T(8,128)(2,1)}), bf16[512,3072]{1,0:T(8,128)(2,1)}) %all-gather.2.cloned.1.call-update) | async-done | bytes 3145744 | tf_op jit(solution)/shard_map/all_gather | solution.py:28
  68.5 32.9 %fusion.4 = bf16[512,3072]{1,0:T(8,128)(2,1)} fusion(bf16[1,2688,3072]{2,1,0:T(8,128)(2,1)} %param.9, bf16[512,3072]{1,0:T(8,128)(2,1)} %all-gather.2.cloned.1.call-done, bf16[1,3072,2688]{2,1,0:T(8,128)(2,1)} %param.8), kind=kOutput, calls=%fused_computation.7 | convolution fusion | flops 16919887872 | bytes 39321600 | tf_op jit(solution)/shard_map/dot_general | solution.py:33
  101.4 0.0 copy-start
  101.4 0.0 reduce-scatter.2.cloned.1.call-update
  101.4 12.2 %reduce-scatter.2.cloned.1.call-done = bf16[512,1536]{1,0:T(8,128)(2,1)} async-done(((bf16[512,3072]{1,0:T(8,128)(2,1)}), bf16[512,1536]{1,0:T(8,128)(2,1)}) %reduce-scatter.2.cloned.1.call-update) | async-done | bytes 1572880 | tf_op jit(solution)/shard_map/reduce_scatter | solution.py:34
  113.6 5.7 %all-to-all-start.1 = ((bf16[8,64,1536]{2,1,0:T(8,128)(2,1)}), bf16[8,64,1536]{2,1,0:T(8,128)(2,1)}, u32[]{:S(2)}, u32[]{:S(2)}) async-start(bf16[8,64,1536]{2,1,0:T(8,128)(2,1)} %bitcast.31), calls=%async_computation.2 | async-start | bytes 3145728 | tf_op jit(solution)/shard_map/all_to_all | solution.py:37
  119.4 0.0 copy-done
  119.4 0.1 copy.10
  119.5 37.5 %all-to-all-done.1 = bf16[8,64,1536]{2,1,0:T(8,128)(2,1)} async-done(((bf16[8,64,1536]{2,1,0:T(8,128)(2,1)}), bf16[8,64,1536]{2,1,0:T(8,128)(2,1)}, u32[]{:S(2)}, u32[]{:S(2)}) %all-to-all-start.1) | async-done | bytes 1572896 | tf_op jit(solution)/shard_map/all_to_all | solution.py:37
  157.0 1.8 %bitcast_convert_fusion = f32[512,1536]{1,0:T(8,128)S(1)} fusion(bf16[8,64,1536]{2,1,0:T(8,128)(2,1)} %all-to-all-done.1), kind=kLoop, calls=%fused_computation.9 | loop fusion | flops 786432 | bytes 4718592 | tf_op jit(solution)/shard_map/convert_element_type | solution.py:39
  158.8 2.3 %gather_fusion = f32[256,1536]{1,0:T(8,128)} fusion(f32[512,1536]{1,0:T(8,128)S(1)} %bitcast_convert_fusion, s32[1024]{0:T(1024)S(1)} %pad_clamp_fusion), kind=kCustom, calls=%fused_computation | custom fusion | bytes 3146752 | tf_op jit(solution)/shard_map/gather | solution.py:40
  161.1 1.8 %reshape.61 = f32[64,4,1536]{2,1,0:T(4,128)S(1)} reshape(f32[256,1536]{1,0:T(8,128)} %gather_fusion) | data formatting | bytes 3145728 | tf_op jit(solution)/shard_map/reshape | solution.py:40
  162.9 1.8 %multiply_reduce_fusion = bf16[64,1536]{1,0:T(8,128)(2,1)} fusion(f32[64,4,1536]{2,1,0:T(4,128)S(1)} %reshape.61, f32[64,4]{1,0:T(8,128)S(1)} %copy.10), kind=kLoop, calls=%fused_computation.10 | loop fusion | flops 688128 | bytes 1770496 | tf_op jit(solution)/shard_map/reduce_sum | solution.py:41
  (5 shorter events, 0.1 us)
Async XLA Ops:
  6.5 62.0 %all-gather.2.cloned.1.call-start = ((), (), s32[]{:S(2)}) async-start(), calls=%async_computation.3 | async-start | bytes 4718592 | tf_op jit(solution)/shard_map/all_gather | solution.py:28
  57.2 56.4 %reduce-scatter.2.cloned.1.call-start = ((), (), s32[]{:S(2)}) async-start(), calls=%async_computation.4 | async-start | bytes 4718592 | tf_op jit(solution)/shard_map/reduce_scatter | solution.py:34
  101.4 18.0 %copy-start = (f32[64,4]{0,1:T(4,128)S(1)}, f32[64,4]{0,1:T(4,128)}, u32[]{:S(2)}) copy-start(f32[64,4]{0,1:T(4,128)} %param.7) | copy-start | bytes 3076
  113.6 43.3 %all-to-all-start.1 = ((bf16[8,64,1536]{2,1,0:T(8,128)(2,1)}), bf16[8,64,1536]{2,1,0:T(8,128)(2,1)}, u32[]{:S(2)}, u32[]{:S(2)}) async-start(bf16[8,64,1536]{2,1,0:T(8,128)(2,1)} %bitcast.31), calls=%async_computation.2 | async-start | bytes 3145728 | tf_op jit(solution)/shard_map/all_to_all | solution.py:37
Sparse Core Ops, SparseCore 0:
  57.3 11.1 all-gather.1
  101.5 12.0 reduce-scatter.1
where the time goes:
time: 172 us
  waiting for transfers between devices  60.8 us (35%)
  blocking collectives  44.2 us (26%)
  matrix products  32.9 us (19%)
  between operations  13.5 us (8%)
  local copies, waits for them, and re-layouts  9.25 us (5%)
  starting transfers between devices  5.97 us (3%)
  other arithmetic  4.98 us (3%)
    all_to_all x1, blocking collectives, body(): lax.all_to_all(jnp.zeros((slot_count, tokens.shape[1]), tokens.dtype).at[...  44.2 us
    all_to_all x1, waiting for transfers between devices, body(): lax.all_to_all(results.astype(jnp.bfloat16), 'expert', split_axis=0, conc...  37.5 us
    dot_general x1, matrix products, body(): jnp.dot(hidden, down_weight, preferred_element_type=jnp.float32)  32.9 us
    reduce_scatter x1, waiting for transfers between devices, body(): lax.psum_scatter(partial_out.astype(jnp.bfloat16), 'tensor', scatter_dime...  12.2 us
    all_gather x1, waiting for transfers between devices, body(): lax.all_gather(arrived, 'tensor', axis=1, tiled=True)  11.1 us
    all_to_all x1, starting transfers between devices, body(): lax.all_to_all(results.astype(jnp.bfloat16), 'expert', split_axis=0, conc...  5.74 us
  transfers between devices with their start and end apart: 3, of which 3 were waited for; matrix products, arithmetic and copies ran while one was open for 0% of the time, Pallas kernels for 0%

commit v1 on v0

v1 whole, which is shorter than its diff:
```python
import jax
import jax.numpy as jnp
from jax import lax
from jax.sharding import PartitionSpec as P


def body(tokens, route_ids, gates, w_up, w_down):
    experts = lax.axis_size("expert")
    ids = jnp.arange(experts, dtype=jnp.int32)
    dense = jnp.sum(
        jnp.where(route_ids[:, :, None] == ids, gates[:, :, None], 0.0), axis=1
    )
    mine = lax.all_to_all(dense.T, "expert", split_axis=0, concat_axis=0, tiled=True).reshape(-1, 1)
    rows = lax.all_gather(tokens, "expert", axis=0, tiled=True)
    rows = lax.all_gather(rows, "tensor", axis=1, tiled=True)
    upward = jnp.dot(rows, w_up[0], preferred_element_type=jnp.float32)
    hidden = jax.nn.silu(upward).astype(jnp.bfloat16)
    out = jnp.dot(hidden, w_down[0], preferred_element_type=jnp.float32) * mine
    half = lax.psum_scatter(out.astype(jnp.bfloat16), "tensor", scatter_dimension=1, tiled=True)
    return lax.psum_scatter(half, "expert", scatter_dimension=0, tiled=True)


def solution(mesh):
    return jax.shard_map(
        body,
        mesh=mesh,
        in_specs=(
            P(("group", "expert"), "tensor"),
            P(("group", "expert"), None),
            P(("group", "expert"), None),
            P("expert", None, "tensor"),
            P("expert", "tensor", None),
        ),
        out_specs=P(("group", "expert"), "tensor"),
        check_vma=False,
    )
```

time: 172 us -> 190 us (1.10)
  waiting for transfers between devices: 60.8 us -> 133 us
  blocking collectives: 44.2 us -> 9.66 us
  local copies, waits for them, and re-layouts: 9.25 us -> 0.59 us
  starting transfers between devices: 5.97 us -> 0.12 us
  other arithmetic: 4.98 us -> 1.37 us
    reduce_scatter x1 -> x2, waiting for transfers between devices: 12.2 us -> 82 us  [the longest x1 69.8 us: body(): return lax.psum_scatter(half, 'expert', scatter_dimension=0, tiled=True)]
    all_gather x1 -> x2, waiting for transfers between devices: 11.1 us -> 50 us  [the longest x1 49.2 us: body(): rows = lax.all_gather(tokens, 'expert', axis=0, tiled=True)]
    all_to_all x1 -> x0, waiting for transfers between devices: 37.5 us -> none  [body(): lax.all_to_all(results.astype(jnp.bfloat16), 'expert', split_axis=0, conc...]
    all_to_all x1, blocking collectives: 44.2 us -> 9.66 us  [body(): lax.all_to_all(dense.T, 'expert', split_axis=0, concat_axis=0, tiled=True)]
    all_to_all x1 -> x0, starting transfers between devices: 5.74 us -> none  [body(): lax.all_to_all(results.astype(jnp.bfloat16), 'expert', split_axis=0, conc...]
    gather x1 -> x0, local copies, waits for them, and re-layouts: 2.34 us -> none  [body(): picked = returned[target].reshape(tok_rows, per_token, -1)]
    scatter x1 -> x0, local copies, waits for them, and re-layouts: 2.33 us -> none  [body(): jnp.zeros((slot_count, tokens.shape[1]), tokens.dtype).at[target]]
    reshape x2 -> x0, local copies, waits for them, and re-layouts: 1.94 us -> none  [the longest x1 1.76 us: body(): picked = returned[target].reshape(tok_rows, per_token, -1)]
  transfers between devices with their start and end apart: 3 -> 4, of which waited for: 3 -> 4; matrix products, arithmetic and copies ran while one was open for 0% -> 1% of each run, Pallas kernels for 0% -> 0%
where the time goes in v1:
time: 190 us
  waiting for transfers between devices  133 us (70%)
  matrix products  32.6 us (17%)
  between operations  13.1 us (7%)
  blocking collectives  9.66 us (5%)
    reduce_scatter x1, waiting for transfers between devices, body(): return lax.psum_scatter(half, 'expert', scatter_dimension=0, tiled=True)  69.8 us
    all_gather x1, waiting for transfers between devices, body(): rows = lax.all_gather(tokens, 'expert', axis=0, tiled=True)  49.2 us
    dot_general x1, matrix products, body(): out = jnp.dot(hidden, w_down[0], preferred_element_type=jnp.float32) * mine  32.6 us
    reduce_scatter x1, waiting for transfers between devices, body(): lax.psum_scatter(out.astype(jnp.bfloat16), 'tensor', scatter_dimension=1,...  12.2 us
    all_to_all x1, blocking collectives, body(): lax.all_to_all(dense.T, 'expert', split_axis=0, concat_axis=0, tiled=True)  9.66 us
  transfers between devices with their start and end apart: 4, of which 4 were waited for; matrix products, arithmetic and copies ran while one was open for 1% of the time, Pallas kernels for 0%

profile of v1, /device:TPU:0, one launch (start us, length us, event | category | flops | bytes accessed | tf_op | source)
XLA Modules:
  0.0 190.2 jit_solution(12326002622731647412)
XLA Ops:
  6.5 0.0 all-gather.3.cloned.1.call-start
  6.5 0.7 all-gather.3.cloned.1.call-update
  7.3 0.0 all-gather.5.cloned.1.call-start
  7.3 49.2 %all-gather.3.cloned.1.call-done = bf16[512,1536]{1,0:T(8,128)(2,1)} async-done(((bf16[64,1536]{1,0:T(8,128)(2,1)}), bf16[512,1536]{1,0:T(8,128)(2,1)}) %all-gather.3.cloned.1.call-update) | async-done | bytes 1572880 | tf_op jit(solution)/shard_map/all_gather | solution.py:14
  56.5 0.0 all-gather.5.cloned.1.call-update
  56.5 0.0 reduce-scatter.3.cloned.1.call-start
  56.5 0.7 select_reduce_fusion
  57.2 9.7 %all_to_all.9 = f32[8,1,64]{2,1,0:T(1,128)S(1)} all-to-all(f32[8,1,64]{2,1,0:T(1,128)S(1)} %bitcast.18), channel_id=1, replica_groups=mesh['group'=2,'expert'=8,'tensor'=2] {'expert'}, dimensions={0} | all-to-all | bytes 4096 | tf_op jit(solution)/shard_map/all_to_all | solution.py:13
  66.9 0.5 broadcast.7
  67.4 0.7 reduce.3
  68.1 0.1 mul.15
  68.2 0.8 all-gather.5.cloned.1.call-done
  69.0 32.6 %multiply_convert_fusion = bf16[512,3072]{1,0:T(8,128)(2,1)} fusion(bf16[1,2688,3072]{2,1,0:T(8,128)(2,1)} %param.9, f32[512]{0:T(512)S(1)} %mul.15, bf16[512,3072]{1,0:T(8,128)(2,1)} %all-gather.5.cloned.1.call-done, bf16[1,3072,2688]{2,1,0:T(8,128)(2,1)} %param.8), kind=kOutput, calls=%fused_computation.4 | convolution fusion | flops 16921460736 | bytes 39323648 | tf_op jit(solution)/shard_map/dot_general | solution.py:18
  101.6 0.0 reduce-scatter.3.cloned.1.call-update
  101.6 0.0 reduce-scatter.5.cloned.1.call-start
  101.7 12.2 %reduce-scatter.3.cloned.1.call-done = bf16[512,1536]{1,0:T(8,128)(2,1)} async-done(((bf16[512,3072]{1,0:T(8,128)(2,1)}), bf16[512,1536]{1,0:T(8,128)(2,1)}) %reduce-scatter.3.cloned.1.call-update) | async-done | bytes 1572880 | tf_op jit(solution)/shard_map/reduce_scatter | solution.py:19
  113.8 0.0 reduce-scatter.5.cloned.1.call-update
  113.9 69.8 %reduce-scatter.5.cloned.1.call-done = bf16[64,1536]{1,0:T(8,128)(2,1)} async-done(((bf16[512,1536]{1,0:T(8,128)(2,1)}), bf16[64,1536]{1,0:T(8,128)(2,1)}) %reduce-scatter.5.cloned.1.call-update) | async-done | bytes 196624 | tf_op jit(solution)/shard_map/reduce_scatter | solution.py:20
Async XLA Ops:
  6.5 49.9 %all-gather.3.cloned.1.call-start = ((), (), s32[]{:S(2)}) async-start(), calls=%async_computation.3 | async-start | bytes 1769472 | tf_op jit(solution)/shard_map/all_gather | solution.py:14
  7.3 61.7 %all-gather.5.cloned.1.call-start = ((), (), s32[]{:S(2)}) async-start(), calls=%async_computation.4 | async-start | bytes 4718592 | tf_op jit(solution)/shard_map/all_gather | solution.py:15
  56.5 57.4 %reduce-scatter.3.cloned.1.call-start = ((), (), s32[]{:S(2)}) async-start(), calls=%async_computation.5 | async-start | bytes 4718592 | tf_op jit(solution)/shard_map/reduce_scatter | solution.py:19
  101.6 82.0 %reduce-scatter.5.cloned.1.call-start = ((), (), s32[]{:S(2)}) async-start(), calls=%async_computation.6 | async-start | bytes 1769472 | tf_op jit(solution)/shard_map/reduce_scatter | solution.py:20
Sparse Core Ops, SparseCore 0:
  9.5 46.8 all-gather.2
  58.0 10.9 all-gather.4
  101.7 12.0 reduce-scatter.2
  117.5 66.1 reduce-scatter.4

commit v2 on v1

v2 whole, which is shorter than its diff:
```python
import jax
import jax.numpy as jnp
from jax import lax
from jax.experimental import pallas as pl
from jax.experimental.pallas import tpu as pltpu
from jax.sharding import PartitionSpec as P

F32, BF16 = jnp.float32, jnp.bfloat16
TILE = 512


def layer_kernel(
    tok, ids, gts, wu_hbm, wd_hbm, out,
    wu, wd, X, H, GS, GR, GB, DS, DR, A, XS, XR, R, CS, CU,
    wu_sem, wd_sem, zs, zr, xs, xr, ds, dr, gs, gr, ds2, dr2, xs2, xr2, chs, chr_,
):
    rows, half = tok.shape
    ff = wu.shape[1]
    pieces = half // TILE
    e, t = lax.axis_index("expert"), lax.axis_index("tensor")
    z, x = e // 2, e % 2
    sib, partner = 1 - t, 2 * z + 1 - x
    interior = (z % 3) > 0
    end = (z % 3) == 0
    order = [z, 1 + z % 2, (2 + 3 * z) % 5, 3 * (1 - z // 2)]

    def remote(src, dst, ss, rs, **dev):
        return pltpu.make_async_remote_copy(
            src, dst, ss, rs, device_id=dev, device_id_type=pl.DeviceIdType.MESH
        )

    def mult(v, m):
        return pl.multiple_of(v, m)

    def block(b):
        return X.at[t, pl.ds(mult(b * rows, rows), rows), :]

    starts = list(range(0, ff, TILE))

    def up_load(j):
        w = min(TILE, ff - starts[j])
        cols = pl.ds(starts[j], w)
        return pltpu.make_async_copy(wu_hbm.at[0, :, cols], wu.at[:, cols], wu_sem.at[j])

    def down_cols(p, own):
        h = t if own else sib
        return pl.ds(mult(h * half + p * TILE, TILE), TILE)

    def down_load(p, own):
        cols = down_cols(p, own)
        return pltpu.make_async_copy(wd_hbm.at[0, :, cols], wd.at[:, cols], wd_sem.at[p, own])

    for j in range(len(starts)):
        up_load(j).start()
    for p in range(pieces):
        down_load(p, 0).start()
        down_load(p, 1).start()

    barrier = pltpu.get_barrier_semaphore()
    for k in range(1, 8):
        pl.semaphore_signal(
            barrier, inc=1, device_id={"expert": (e + k) % 8}, device_id_type=pl.DeviceIdType.MESH
        )
    pl.semaphore_signal(barrier, inc=1, device_id={"tensor": sib}, device_id_type=pl.DeviceIdType.MESH)
    pl.semaphore_wait(barrier, 8)

    def z_send(s):
        return remote(tok, block(e), zs.at[s], zr.at[z], expert=order[s] * 2 + x)

    def z_recv(s):
        return remote(tok, block(order[s] * 2 + x), zs.at[s], zr.at[order[s]], expert=e)

    def x_copy(s):
        b = order[s] * 2 + x
        return remote(tok if s == 0 else block(b), block(b), xs.at[s], xr.at[s], expert=partner)

    def d_copy(s, j):
        b = order[s] * 2 + (x if j == 0 else 1 - x)
        src = tok if s == 0 and j == 0 else block(b)
        return remote(src, block(b), ds.at[s, j], dr.at[s, j], tensor=sib)

    def forward_a(s):
        if s:
            z_recv(s).wait_recv()
        x_copy(s).start()
        d_copy(s, 0).start()

    def forward_b(s):
        x_copy(s).wait_recv()
        d_copy(s, 1).start()

    def forward_c(s):
        d_copy(s, 0).wait_recv()
        d_copy(s, 1).wait_recv()

    forward_a(0)
    for s in (1, 2, 3):
        z_send(s).start()
    X[t, pl.ds(mult(e * rows, rows), rows), :] = tok[...]

    lane = lax.broadcasted_iota(jnp.int32, (rows, 128), 1)
    dense = jnp.zeros((rows, 128), F32)
    for k in range(ids.shape[1]):
        dense = dense + jnp.where(ids[:, k : k + 1] == lane, gts[:, k : k + 1], 0.0)
    dense = jnp.concatenate([dense, jnp.zeros((128 - rows, 128), F32)], axis=0)
    GS[...] = dense.T[0:8, :]
    GR[e] = GS[...]

    def g_copy(k):
        return remote(GS, GR.at[e], gs.at[k], gr.at[e], expert=(e + k) % 8)

    def g_recv(k):
        o = (e + k) % 8
        return remote(GS, GR.at[o], gs.at[k], gr.at[o], expert=o)

    for k in range(1, 8):
        g_copy(k).start()
    forward_a(1)
    for k in range(1, 8):
        g_recv(k).wait_recv()
    mine = lax.broadcasted_iota(jnp.int32, (8, 128), 0) == e

    @pl.loop(0, 8)
    def _(b):
        row = jnp.sum(jnp.where(mine, GR[b], 0.0), axis=0, keepdims=True)
        full = jnp.broadcast_to(row, (128, 128)).T
        GB[pl.ds(mult(b * rows, rows), rows), :] = full[0:rows, :]

    def up(s):
        rs = pl.ds(mult(order[s] * 2 * rows, 2 * rows), 2 * rows)

        def tile(cols):
            v = jnp.dot(X[0, rs, :], wu[0:half, cols], preferred_element_type=F32)
            v = v + jnp.dot(X[1, rs, :], wu[half : 2 * half, cols], preferred_element_type=F32)
            H[:, cols] = (v / (1.0 + jnp.exp(-v))).astype(BF16)

        full = ff // TILE
        if s == 0:
            @pl.loop(0, full)
            def _(j):
                cols = pl.ds(mult(j * TILE, TILE), TILE)
                pltpu.make_async_copy(wu_hbm.at[0, :, cols], wu.at[:, cols], wu_sem.at[j]).wait()
                tile(cols)
        else:
            @pl.loop(0, full)
            def _(j):
                tile(pl.ds(mult(j * TILE, TILE), TILE))
        if ff % TILE:
            if s == 0:
                up_load(full).wait()
            tile(pl.ds(full * TILE, ff % TILE))

    def d2(q):
        return remote(DS.at[q], DR.at[q], ds2.at[q], dr2.at[q], tensor=sib)

    def x2(q):
        return remote(XS.at[q], XR.at[q], xs2.at[q], xr2.at[q], expert=partner)

    def chain(q, c, u, p):
        return remote(CS.at[q], CU.at[u, c, p], chs.at[q], chr_.at[u, c, p], expert=e + 4 * u - 2)

    mine_rows = pl.ds(mult(x * rows, rows), rows)
    other_rows = pl.ds(mult((1 - x) * rows, rows), rows)

    def stage_b(q):
        d2(q).wait_recv()
        XS[q] = (A[q, other_rows, :] + DR[q, other_rows, :].astype(F32)).astype(BF16)
        x2(q).start()
        R[q] = A[q, mine_rows, :] + DR[q, mine_rows, :].astype(F32)

    def stage_c(q):
        x2(q).wait_recv()
        r = R[q] + XR[q].astype(F32)
        R[q] = r
        s, p = q // pieces, q % pieces

        @pl.when(end & (q >= pieces))
        def _():
            CS[q] = r.astype(BF16)
            chain(q, z + s * (1 - 2 * (z // 3)), 1 - z // 3, p).start()

    def down(s):
        rs = pl.ds(mult(order[s] * 2 * rows, 2 * rows), 2 * rows)

        @pl.loop(0, pieces)
        def _(p):
            q = s * pieces + p
            gate = jnp.concatenate([GB[rs, :]] * (TILE // 128), axis=1)
            if s == 0:
                down_load(p, 0).wait()
            v = jnp.dot(H[...], wd[:, down_cols(p, 0)], preferred_element_type=F32)
            DS[q] = (v * gate).astype(BF16)
            d2(q).start()
            if s == 0:
                down_load(p, 1).wait()
            v = jnp.dot(H[...], wd[:, down_cols(p, 1)], preferred_element_type=F32)
            A[q] = v * gate
            pl.when(q >= 1)(lambda: stage_b(q - 1))
            pl.when(q >= 2)(lambda: stage_c(q - 2))

    forward_b(0)
    forward_c(0)
    for s in range(4):
        up(s)
        if s + 2 < 4:
            forward_a(s + 2)
        if s + 1 < 4:
            forward_b(s + 1)
        down(s)
        if s + 1 < 4:
            forward_c(s + 1)
    last = 4 * pieces - 1
    stage_b(last)
    stage_c(last - 1)
    stage_c(last)

    @pl.when(interior)
    def _():
        for s in (1, 3, 2):
            c, u = order[s], (1 - z % 2) if s == 2 else (1 - z // 2)

            @pl.loop(0, pieces)
            def _(p):
                q = s * pieces + p
                remote(CS.at[q], CU.at[u, c, p], chs.at[q], chr_.at[u, c, p], expert=e).wait_recv()
                CS[q] = (R[q] + CU[u, c, p].astype(F32)).astype(BF16)
                chain(q, c, u, p).start()

    for p in range(pieces):
        for u, there in ((1, z > 0), (0, z < 3)):
            @pl.when(there)
            def _():
                remote(CS.at[p], CU.at[u, z, p], chs.at[p], chr_.at[u, z, p], expert=e).wait_recv()
                R[p] += CU[u, z, p].astype(F32)
        out[:, p * TILE : (p + 1) * TILE] = R[p].astype(BF16)

    for s in range(4):
        if s:
            z_send(s).wait_send()
        x_copy(s).wait_send()
        d_copy(s, 0).wait_send()
        d_copy(s, 1).wait_send()
    for k in range(1, 8):
        g_copy(k).wait_send()

    @pl.loop(0, 4 * pieces)
    def _(q):
        d2(q).wait_send()
        x2(q).wait_send()

    @pl.loop(pieces, 4 * pieces)
    def _(q):
        remote(CS.at[q], CU.at[0, 0, 0], chs.at[q], chr_.at[0, 0, 0], expert=e).wait_send()


def fused(tokens, route_ids, gates, w_up, w_down):
    rows, half = tokens.shape
    d, ff = w_up.shape[1:]
    pieces = half // TILE
    q = 4 * pieces
    dma = pltpu.SemaphoreType.DMA
    vmem = pl.BlockSpec(memory_space=pltpu.VMEM)
    hbm = pl.BlockSpec(memory_space=pl.ANY)
    return pl.pallas_call(
        layer_kernel,
        out_shape=jax.ShapeDtypeStruct((rows, half), BF16),
        in_specs=[vmem, vmem, vmem, hbm, hbm],
        out_specs=vmem,
        scratch_shapes=[
            pltpu.VMEM((d, ff), BF16),
            pltpu.VMEM((ff, d), BF16),
            pltpu.VMEM((2, 8 * rows, half), BF16),
            pltpu.VMEM((2 * rows, ff), BF16),
            pltpu.VMEM((8, 128), F32),
            pltpu.VMEM((8, 8, 128), F32),
            pltpu.VMEM((8 * rows, 128), F32),
            pltpu.VMEM((q, 2 * rows, TILE), BF16),
            pltpu.VMEM((q, 2 * rows, TILE), BF16),
            pltpu.VMEM((q, 2 * rows, TILE), F32),
            pltpu.VMEM((q, rows, TILE), BF16),
            pltpu.VMEM((q, rows, TILE), BF16),
            pltpu.VMEM((q, rows, TILE), F32),
            pltpu.VMEM((q, rows, TILE), BF16),
            pltpu.VMEM((2, 4, pieces, rows, TILE), BF16),
            dma((pl.cdiv(ff, TILE),)),
            dma((pieces, 2)),
            dma((4,)), dma((4,)), dma((4,)), dma((4,)),
            dma((4, 2)), dma((4, 2)),
            dma((8,)), dma((8,)),
            dma((q,)), dma((q,)), dma((q,)), dma((q,)),
            dma((q,)), dma((2, 4, pieces)),
        ],
        compiler_params=pltpu.CompilerParams(
            collective_id=0, has_side_effects=True, vmem_limit_bytes=60 * 2**20
        ),
    )(tokens, route_ids, gates, w_up, w_down)


def general(tokens, route_ids, gates, w_up, w_down):
    experts = lax.axis_size("expert")
    tok_rows, per_token = route_ids.shape
    capacity = min(tok_rows, 2 * tok_rows * per_token // experts)
    flat_ids = route_ids.reshape(-1)
    onehot = (flat_ids[:, None] == jnp.arange(experts, dtype=jnp.int32)[None, :]).astype(jnp.int32)
    within = jnp.sum((jnp.cumsum(onehot, axis=0) - onehot) * onehot, axis=1)
    target = flat_ids * capacity + within
    slots = jnp.zeros((experts * capacity, tokens.shape[1]), tokens.dtype)
    slots = slots.at[target].set(jnp.repeat(tokens, per_token, axis=0))
    arrived = lax.all_to_all(slots, "expert", split_axis=0, concat_axis=0, tiled=True)
    arrived = lax.all_gather(arrived, "tensor", axis=1, tiled=True)
    upward = jnp.dot(arrived, w_up[0], preferred_element_type=F32)
    hidden = jax.nn.silu(upward).astype(BF16)
    partial = jnp.dot(hidden, w_down[0], preferred_element_type=F32).astype(BF16)
    results = lax.psum_scatter(partial, "tensor", scatter_dimension=1, tiled=True)
    returned = lax.all_to_all(results, "expert", split_axis=0, concat_axis=0, tiled=True)
    picked = returned[target].reshape(tok_rows, per_token, -1).astype(F32)
    return jnp.sum(picked * gates[:, :, None], axis=1).astype(BF16)


def solution(mesh):
    def body(tokens, route_ids, gates, w_up, w_down):
        rows, half = tokens.shape
        fits = mesh.shape["expert"] == 8 and mesh.shape["tensor"] == 2
        fits = fits and rows == 64 and half % TILE == 0 and w_up.shape[2] % 128 == 0
        form = fused if fits else general
        return form(tokens, route_ids, gates, w_up, w_down)

    return jax.shard_map(
        body,
        mesh=mesh,
        in_specs=(
            P(("group", "expert"), "tensor"),
            P(("group", "expert"), None),
            P(("group", "expert"), None),
            P("expert", None, "tensor"),
            P("expert", "tensor", None),
        ),
        out_specs=P(("group", "expert"), "tensor"),
        check_vma=False,
    )
```

time: 190 us -> 94.2 us (0.50)
  waiting for transfers between devices: 133 us -> 0 us
  Pallas kernels: 0 us -> 89.6 us
  matrix products: 32.6 us -> 0 us
  between operations: 13.1 us -> 0.01 us
  blocking collectives: 9.66 us -> 0 us
  local copies, waits for them, and re-layouts: 0.59 us -> 4.37 us
    pallas_call x0 -> x1, Pallas kernels: none -> 89.6 us  [fused(): pl.pallas_call(layer_kernel, out_shape=jax.ShapeDtypeStruct((rows, half),...]
    reduce_scatter x2 -> x0, waiting for transfers between devices: 82 us -> none  [the longest x1 69.8 us: body(): return lax.psum_scatter(half, 'expert', scatter_dimension=0, tiled=True)]
    all_gather x2 -> x0, waiting for transfers between devices: 50 us -> none  [the longest x1 49.2 us: body(): rows = lax.all_gather(tokens, 'expert', axis=0, tiled=True)]
    dot_general x1 -> x0, matrix products: 32.6 us -> none  [body(): out = jnp.dot(hidden, w_down[0], preferred_element_type=jnp.float32) * mine]
    all_to_all x1 -> x0, blocking collectives: 9.66 us -> none  [body(): lax.all_to_all(dense.T, 'expert', split_axis=0, concat_axis=0, tiled=True)]
    unnamed x0 -> x3, local copies, waits for them, and re-layouts: none -> 4.37 us
  transfers between devices with their start and end apart: 4 -> 0, of which waited for: 4 -> 0; matrix products, arithmetic and copies ran while one was open for 1% -> 0% of each run, Pallas kernels for 0% -> 0%
where the time goes in v2:
time: 94.2 us; the launch traced here: 94 us
  Pallas kernels  89.6 us (95%)
  local copies, waits for them, and re-layouts  4.37 us (5%)
    pallas_call x1, Pallas kernels, fused(): pl.pallas_call(layer_kernel, out_shape=jax.ShapeDtypeStruct((rows, half),...  89.6 us
    unnamed x3, local copies, waits for them, and re-layouts  4.37 us

profile of v2, /device:TPU:0, one launch (start us, length us, event | category | flops | bytes accessed | tf_op | source)
XLA Modules:
  0.0 94.0 jit_solution(2574950193115640744)
XLA Ops:
  0.0 1.4 %copy.6.ids = s32[64,4]{1,0:T(8,128)} copy(s32[64,4]{0,1:T(4,128)} %param.6) | data formatting | bytes 2048 | tf_op args[1]
  1.4 1.4 %copy.7.gts = f32[64,4]{1,0:T(8,128)} copy(f32[64,4]{0,1:T(4,128)} %param.7) | data formatting | bytes 2048 | tf_op args[2]
  2.8 89.6 %shard_map.55 = bf16[64,1536]{1,0:T(8,128)(2,1)} custom-call(bf16[64,1536]{1,0:T(8,128)(2,1)} %tok.1, s32[64,4]{1,0:T(8,128)} %copy.6.ids, f32[64,4]{1,0:T(8,128)} %copy.7.gts, bf16[1,3072,2688]{2,1,0:T(8,128)(2,1)} %wu_hbm.1, bf16[1,2688,3072]{2,1,0:T(8,128)(2,1)} %wd_hbm.1), custom_call_target="tpu_custom_call" | custom-call | tf_op jit(solution)/shard_map/pallas_call | solution.py:264
  92.4 1.6 %copy.9 = bf16[64,1536]{1,0:T(8,128)(2,1)} copy(bf16[64,1536]{1,0:T(8,128)(2,1)} %shard_map.55) | data formatting | bytes 393216

commit v3 on v2

--- a/solution.py
+++ b/solution.py
@@ -22,7 +22,7 @@
     sib, partner = 1 - t, 2 * z + 1 - x
     interior = (z % 3) > 0
     end = (z % 3) == 0
-    order = [z, 1 + z % 2, (2 + 3 * z) % 5, 3 * (1 - z // 2)]
+    pairs = [z // 2, 1 - z // 2]
 
     def remote(src, dst, ss, rs, **dev):
         return pltpu.make_async_remote_copy(
@@ -64,38 +64,47 @@
     pl.semaphore_signal(barrier, inc=1, device_id={"tensor": sib}, device_id_type=pl.DeviceIdType.MESH)
     pl.semaphore_wait(barrier, 8)
 
-    def z_send(s):
-        return remote(tok, block(e), zs.at[s], zr.at[z], expert=order[s] * 2 + x)
-
-    def z_recv(s):
-        return remote(tok, block(order[s] * 2 + x), zs.at[s], zr.at[order[s]], expert=e)
-
-    def x_copy(s):
-        b = order[s] * 2 + x
-        return remote(tok if s == 0 else block(b), block(b), xs.at[s], xr.at[s], expert=partner)
-
-    def d_copy(s, j):
-        b = order[s] * 2 + (x if j == 0 else 1 - x)
-        src = tok if s == 0 and j == 0 else block(b)
-        return remote(src, block(b), ds.at[s, j], dr.at[s, j], tensor=sib)
-
-    def forward_a(s):
-        if s:
-            z_recv(s).wait_recv()
-        x_copy(s).start()
-        d_copy(s, 0).start()
-
-    def forward_b(s):
-        x_copy(s).wait_recv()
-        d_copy(s, 1).start()
-
-    def forward_c(s):
-        d_copy(s, 0).wait_recv()
-        d_copy(s, 1).wait_recv()
-
-    forward_a(0)
-    for s in (1, 2, 3):
-        z_send(s).start()
+    def z_copy(c, up):
+        src = block(c * 2 + x)
+        return remote(src, src, zs.at[c, up], zr.at[c], expert=e + 4 * up - 2)
+
+    def x_copy(c, src=None):
+        b = block(c * 2 + x)
+        return remote(b if src is None else src, b, xs.at[c], xr.at[c], expert=partner)
+
+    def x_recv(c):
+        x_copy(c).wait_recv()
+
+    def d_copy(c, j, src=None):
+        b = block(c * 2 + (x if j == 0 else 1 - x))
+        return remote(b if src is None else src, b, ds.at[c, j], dr.at[c, j], tensor=sib)
+
+    def own_send(up):
+        return remote(tok, block(e), zs.at[z, up], zr.at[z], expert=e + 4 * up - 2)
+
+    def arrive(h):
+        for up in (1, 0):
+            c = z - h if up else z + h
+
+            @pl.when((c >= 0) if up else (c <= 3))
+            def _():
+                z_copy(c, up).wait_recv()
+                pl.when((z < 3) if up else (z > 0))(lambda: z_copy(c, up).start())
+                x_copy(c).start()
+                d_copy(c, 0).start()
+
+    def crossed(c):
+        x_recv(c)
+        d_copy(c, 1).start()
+
+    def ready(c):
+        d_copy(c, 0).wait_recv()
+        d_copy(c, 1).wait_recv()
+
+    pl.when(z < 3)(lambda: own_send(1).start())
+    pl.when(z > 0)(lambda: own_send(0).start())
+    x_copy(z, tok).start()
+    d_copy(z, 0, tok).start()
     X[t, pl.ds(mult(e * rows, rows), rows), :] = tok[...]
 
     lane = lax.broadcasted_iota(jnp.int32, (rows, 128), 1)
@@ -115,7 +124,8 @@
 
     for k in range(1, 8):
         g_copy(k).start()
-    forward_a(1)
+    arrive(1)
+    crossed(z)
     for k in range(1, 8):
         g_recv(k).wait_recv()
     mine = lax.broadcasted_iota(jnp.int32, (8, 128), 0) == e
@@ -127,7 +137,7 @@
         GB[pl.ds(mult(b * rows, rows), rows), :] = full[0:rows, :]
 
     def up(s):
-        rs = pl.ds(mult(order[s] * 2 * rows, 2 * rows), 2 * rows)
+        rs = pl.ds(mult(pairs[s] * 4 * rows, 4 * rows), 4 * rows)
 
         def tile(cols):
             v = jnp.dot(X[0, rs, :], wu[0:half, cols], preferred_element_type=F32)
@@ -156,31 +166,40 @@
     def x2(q):
         return remote(XS.at[q], XR.at[q], xs2.at[q], xr2.at[q], expert=partner)
 
-    def chain(q, c, u, p):
-        return remote(CS.at[q], CU.at[u, c, p], chs.at[q], chr_.at[u, c, p], expert=e + 4 * u - 2)
-
-    mine_rows = pl.ds(mult(x * rows, rows), rows)
-    other_rows = pl.ds(mult((1 - x) * rows, rows), rows)
+    def chain(q, i, c, u, p):
+        return remote(
+            CS.at[q, i], CU.at[u, c, p], chs.at[q, i], chr_.at[u, c, p], expert=e + 4 * u - 2
+        )
+
+    def part(i, of):
+        return pl.ds(mult((2 * i + of) * rows, rows), rows)
 
     def stage_b(q):
         d2(q).wait_recv()
-        XS[q] = (A[q, other_rows, :] + DR[q, other_rows, :].astype(F32)).astype(BF16)
+        for i in range(2):
+            rs = part(i, 1 - x)
+            XS[q, i] = (A[q, rs, :] + DR[q, rs, :].astype(F32)).astype(BF16)
         x2(q).start()
-        R[q] = A[q, mine_rows, :] + DR[q, mine_rows, :].astype(F32)
+        for i in range(2):
+            rs = part(i, x)
+            R[q, i] = A[q, rs, :] + DR[q, rs, :].astype(F32)
 
     def stage_c(q):
         x2(q).wait_recv()
-        r = R[q] + XR[q].astype(F32)
-        R[q] = r
         s, p = q // pieces, q % pieces
-
-        @pl.when(end & (q >= pieces))
-        def _():
-            CS[q] = r.astype(BF16)
-            chain(q, z + s * (1 - 2 * (z // 3)), 1 - z // 3, p).start()
+        for i in range(2):
+            r = R[q, i] + XR[q, i].astype(F32)
+            R[q, i] = r
+            kind = (z + i) % 2 + 2 * s
+
+            @pl.when(end & (kind >= 1))
+            def _():
+                CS[q, i] = r.astype(BF16)
+                pair = z // 2 + s * (1 - 2 * (z // 2))
+                chain(q, i, 2 * pair + i, 1 - z // 2, p).start()
 
     def down(s):
-        rs = pl.ds(mult(order[s] * 2 * rows, 2 * rows), 2 * rows)
+        rs = pl.ds(mult(pairs[s] * 4 * rows, 4 * rows), 4 * rows)
 
         @pl.loop(0, pieces)
         def _(p):
@@ -198,66 +217,81 @@
             pl.when(q >= 1)(lambda: stage_b(q - 1))
             pl.when(q >= 2)(lambda: stage_c(q - 2))
 
-    forward_b(0)
-    forward_c(0)
-    for s in range(4):
-        up(s)
-        if s + 2 < 4:
-            forward_a(s + 2)
-        if s + 1 < 4:
-            forward_b(s + 1)
-        down(s)
-        if s + 1 < 4:
-            forward_c(s + 1)
-    last = 4 * pieces - 1
+    near = z + 1 - 2 * (z % 2)
+    far = [pairs[1] * 2 + z // 2, pairs[1] * 2 + 1 - z // 2]
+    arrive(2)
+    crossed(near)
+    ready(z)
+    ready(near)
+    up(0)
+    arrive(3)
+    crossed(far[0])
+    down(0)
+    crossed(far[1])
+    ready(far[0])
+    ready(far[1])
+    up(1)
+    down(1)
+    last = 2 * pieces - 1
     stage_b(last)
     stage_c(last - 1)
     stage_c(last)
 
+    def pass_on(q, i, c, u, p):
+        remote(CS.at[q, i], CU.at[u, c, p], chs.at[q, i], chr_.at[u, c, p], expert=e).wait_recv()
+        CS[q, i] = (R[q, i] + CU[u, c, p].astype(F32)).astype(BF16)
+        chain(q, i, c, u, p).start()
+
     @pl.when(interior)
     def _():
-        for s in (1, 3, 2):
-            c, u = order[s], (1 - z % 2) if s == 2 else (1 - z // 2)
-
-            @pl.loop(0, pieces)
-            def _(p):
-                q = s * pieces + p
-                remote(CS.at[q], CU.at[u, c, p], chs.at[q], chr_.at[u, c, p], expert=e).wait_recv()
-                CS[q] = (R[q] + CU[u, c, p].astype(F32)).astype(BF16)
-                chain(q, c, u, p).start()
+        @pl.loop(0, pieces)
+        def _(p):
+            for k in (1, 0):
+                pass_on(pieces + p, far[k] % 2, far[k], 1 - z // 2, p)
+
+        @pl.loop(0, pieces)
+        def _(p):
+            pass_on(p, near % 2, near, z // 2, p)
 
     for p in range(pieces):
         for u, there in ((1, z > 0), (0, z < 3)):
             @pl.when(there)
             def _():
-                remote(CS.at[p], CU.at[u, z, p], chs.at[p], chr_.at[u, z, p], expert=e).wait_recv()
-                R[p] += CU[u, z, p].astype(F32)
-        out[:, p * TILE : (p + 1) * TILE] = R[p].astype(BF16)
-
-    for s in range(4):
-        if s:
-            z_send(s).wait_send()
-        x_copy(s).wait_send()
-        d_copy(s, 0).wait_send()
-        d_copy(s, 1).wait_send()
+                remote(CS.at[p, 0], CU.at[u, z, p], chs.at[p, 0], chr_.at[u, z, p], expert=e).wait_recv()
+                R[p, z % 2] += CU[u, z, p].astype(F32)
+        out[:, p * TILE : (p + 1) * TILE] = R[p, z % 2].astype(BF16)
+
+    pl.when(z < 3)(lambda: own_send(1).wait_send())
+    pl.when(z > 0)(lambda: own_send(0).wait_send())
+    for h in (1, 2, 3):
+        pl.when((z - h >= 0) & (z < 3))(lambda: z_copy(z - h, 1).wait_send())
+        pl.when((z + h <= 3) & (z > 0))(lambda: z_copy(z + h, 0).wait_send())
+    for c in range(4):
+        x_copy(c).wait_send()
+        d_copy(c, 0).wait_send()
+        d_copy(c, 1).wait_send()
     for k in range(1, 8):
         g_copy(k).wait_send()
 
-    @pl.loop(0, 4 * pieces)
+    @pl.loop(0, 2 * pieces)
     def _(q):
         d2(q).wait_send()
         x2(q).wait_send()
 
-    @pl.loop(pieces, 4 * pieces)
-    def _(q):
-        remote(CS.at[q], CU.at[0, 0, 0], chs.at[q], chr_.at[0, 0, 0], expert=e).wait_send()
+    def sent(q, i):
+        remote(CS.at[q, i], CU.at[0, 0, 0], chs.at[q, i], chr_.at[0, 0, 0], expert=e).wait_send()
+
+    for p in range(pieces):
+        sent(p, 1 - z % 2)
+        sent(pieces + p, 0)
+        sent(pieces + p, 1)
 
 
 def fused(tokens, route_ids, gates, w_up, w_down):
     rows, half = tokens.shape
     d, ff = w_up.shape[1:]
     pieces = half // TILE
-    q = 4 * pieces
+    q = 2 * pieces
     dma = pltpu.SemaphoreType.DMA
     vmem = pl.BlockSpec(memory_space=pltpu.VMEM)
     hbm = pl.BlockSpec(memory_space=pl.ANY)
@@ -270,25 +304,25 @@
             pltpu.VMEM((d, ff), BF16),
             pltpu.VMEM((ff, d), BF16),
             pltpu.VMEM((2, 8 * rows, half), BF16),
-            pltpu.VMEM((2 * rows, ff), BF16),
+            pltpu.VMEM((4 * rows, ff), BF16),
             pltpu.VMEM((8, 128), F32),
             pltpu.VMEM((8, 8, 128), F32),
             pltpu.VMEM((8 * rows, 128), F32),
-            pltpu.VMEM((q, 2 * rows, TILE), BF16),
-            pltpu.VMEM((q, 2 * rows, TILE), BF16),
-            pltpu.VMEM((q, 2 * rows, TILE), F32),
-            pltpu.VMEM((q, rows, TILE), BF16),
-            pltpu.VMEM((q, rows, TILE), BF16),
-            pltpu.VMEM((q, rows, TILE), F32),
-            pltpu.VMEM((q, rows, TILE), BF16),
+            pltpu.VMEM((q, 4 * rows, TILE), BF16),
+            pltpu.VMEM((q, 4 * rows, TILE), BF16),
+            pltpu.VMEM((q, 4 * rows, TILE), F32),
+            pltpu.VMEM((q, 2, rows, TILE), BF16),
+            pltpu.VMEM((q, 2, rows, TILE), BF16),
+            pltpu.VMEM((q, 2, rows, TILE), F32),
+            pltpu.VMEM((q, 2, rows, TILE), BF16),
             pltpu.VMEM((2, 4, pieces, rows, TILE), BF16),
             dma((pl.cdiv(ff, TILE),)),
             dma((pieces, 2)),
-            dma((4,)), dma((4,)), dma((4,)), dma((4,)),
+            dma((4, 2)), dma((4,)), dma((4,)), dma((4,)),
             dma((4, 2)), dma((4, 2)),
             dma((8,)), dma((8,)),
             dma((q,)), dma((q,)), dma((q,)), dma((q,)),
-            dma((q,)), dma((2, 4, pieces)),
+            dma((q, 2)), dma((2, 4, pieces)),
         ],
         compiler_params=pltpu.CompilerParams(
             collective_id=0, has_side_effects=True, vmem_limit_bytes=60 * 2**20

time: 94.2 us -> 79.7 us (0.85)
  Pallas kernels: 89.6 us -> 75.1 us
    pallas_call x1, Pallas kernels: 89.6 us -> 75.1 us  [fused(): pl.pallas_call(layer_kernel, out_shape=jax.ShapeDtypeStruct((rows, half),...]
where the time goes in v3:
time: 79.7 us; the launch traced here: 79.5 us
  Pallas kernels  75.1 us (94%)
  local copies, waits for them, and re-layouts  4.37 us (5%)
    pallas_call x1, Pallas kernels, fused(): pl.pallas_call(layer_kernel, out_shape=jax.ShapeDtypeStruct((rows, half),...  75.1 us
    unnamed x3, local copies, waits for them, and re-layouts  4.37 us

profile of v3, /device:TPU:0, one launch (start us, length us, event | category | flops | bytes accessed | tf_op | source)
XLA Modules:
  0.0 79.5 jit_solution(17111181786928660088)
XLA Ops:
  0.0 1.4 %copy.6.ids = s32[64,4]{1,0:T(8,128)} copy(s32[64,4]{0,1:T(4,128)} %param.6) | data formatting | bytes 2048 | tf_op args[1]
  1.4 1.4 %copy.7.gts = f32[64,4]{1,0:T(8,128)} copy(f32[64,4]{0,1:T(4,128)} %param.7) | data formatting | bytes 2048 | tf_op args[2]
  2.8 75.1 %shard_map.55 = bf16[64,1536]{1,0:T(8,128)(2,1)} custom-call(bf16[64,1536]{1,0:T(8,128)(2,1)} %tok.1, s32[64,4]{1,0:T(8,128)} %copy.6.ids, f32[64,4]{1,0:T(8,128)} %copy.7.gts, bf16[1,3072,2688]{2,1,0:T(8,128)(2,1)} %wu_hbm.1, bf16[1,2688,3072]{2,1,0:T(8,128)(2,1)} %wd_hbm.1), custom_call_target="tpu_custom_call" | custom-call | tf_op jit(solution)/shard_map/pallas_call | solution.py:298
  77.9 1.6 %copy.9 = bf16[64,1536]{1,0:T(8,128)(2,1)} copy(bf16[64,1536]{1,0:T(8,128)(2,1)} %shard_map.55) | data formatting | bytes 393216

commit v4 on v3

--- a/solution.py
+++ b/solution.py
@@ -107,12 +107,11 @@
     d_copy(z, 0, tok).start()
     X[t, pl.ds(mult(e * rows, rows), rows), :] = tok[...]
 
-    lane = lax.broadcasted_iota(jnp.int32, (rows, 128), 1)
-    dense = jnp.zeros((rows, 128), F32)
-    for k in range(ids.shape[1]):
-        dense = dense + jnp.where(ids[:, k : k + 1] == lane, gts[:, k : k + 1], 0.0)
-    dense = jnp.concatenate([dense, jnp.zeros((128 - rows, 128), F32)], axis=0)
-    GS[...] = dense.T[0:8, :]
+    expert_row = lax.broadcasted_iota(jnp.int32, (8, rows), 0)
+    dense = jnp.zeros((8, rows), F32)
+    for k in range(ids.shape[0]):
+        dense = dense + jnp.where(ids[k : k + 1, :] == expert_row, gts[k : k + 1, :], 0.0)
+    GS[...] = jnp.concatenate([dense, jnp.zeros((8, 128 - rows), F32)], axis=1)
     GR[e] = GS[...]
 
     def g_copy(k):
@@ -232,26 +231,28 @@
     ready(far[1])
     up(1)
     down(1)
-    last = 2 * pieces - 1
-    stage_b(last)
-    stage_c(last - 1)
-    stage_c(last)
-
     def pass_on(q, i, c, u, p):
         remote(CS.at[q, i], CU.at[u, c, p], chs.at[q, i], chr_.at[u, c, p], expert=e).wait_recv()
         CS[q, i] = (R[q, i] + CU[u, c, p].astype(F32)).astype(BF16)
         chain(q, i, c, u, p).start()
 
-    @pl.when(interior)
-    def _():
-        @pl.loop(0, pieces)
-        def _(p):
+    def pass_far(p):
+        @pl.when(interior)
+        def _():
             for k in (1, 0):
                 pass_on(pieces + p, far[k] % 2, far[k], 1 - z // 2, p)
 
-        @pl.loop(0, pieces)
-        def _(p):
-            pass_on(p, near % 2, near, z // 2, p)
+    def pass_near(p):
+        pl.when(interior)(lambda: pass_on(p, near % 2, near, z // 2, p))
+
+    stage_b(2 * pieces - 1)
+    for p in range(pieces):
+        if p >= pieces - 2:
+            stage_c(pieces + p)
+        pass_far(p)
+        if p:
+            pass_near(p - 1)
+    pass_near(pieces - 1)
 
     for p in range(pieces):
         for u, there in ((1, z > 0), (0, z < 3)):
@@ -327,7 +328,7 @@
         compiler_params=pltpu.CompilerParams(
             collective_id=0, has_side_effects=True, vmem_limit_bytes=60 * 2**20
         ),
-    )(tokens, route_ids, gates, w_up, w_down)
+    )(tokens, route_ids.T, gates.T, w_up, w_down)
 
 
 def general(tokens, route_ids, gates, w_up, w_down):

time: 79.7 us -> 72.7 us (0.912)
  Pallas kernels: 75.1 us -> 71 us
  local copies, waits for them, and re-layouts: 4.37 us -> 1.62 us
    pallas_call x1, Pallas kernels: 75.1 us -> 71 us  [fused(): pl.pallas_call(layer_kernel, out_shape=jax.ShapeDtypeStruct((rows, half),...]
    unnamed x3 -> x1, local copies, waits for them, and re-layouts: 4.37 us -> 1.62 us
where the time goes in v4:
time: 72.7 us; the launch traced here: 72.6 us
  Pallas kernels  71 us (98%)
  local copies, waits for them, and re-layouts  1.62 us (2%)
    pallas_call x1, Pallas kernels, fused(): pl.pallas_call(layer_kernel, out_shape=jax.ShapeDtypeStruct((rows, half),...  71 us
    unnamed x1, local copies, waits for them, and re-layouts  1.62 us

profile of v4, /device:TPU:0, one launch (start us, length us, event | category | flops | bytes accessed | tf_op | source)
XLA Modules:
  0.0 72.6 jit_solution(3086138086692149128)
XLA Ops:
  0.0 71.0 %shard_map.55 = bf16[64,1536]{1,0:T(8,128)(2,1)} custom-call(bf16[64,1536]{1,0:T(8,128)(2,1)} %tok.1, s32[4,64]{1,0:T(4,128)} %bitcast.2, f32[4,64]{1,0:T(4,128)} %bitcast.3, bf16[1,3072,2688]{2,1,0:T(8,128)(2,1)} %wu_hbm.1, bf16[1,2688,3072]{2,1,0:T(8,128)(2,1)} %wd_hbm.1), custom_call_target="tpu_custom_call" | custom-call | tf_op jit(solution)/shard_map/pallas_call | solution.py:299
  71.0 1.6 %copy.7 = bf16[64,1536]{1,0:T(8,128)(2,1)} copy(bf16[64,1536]{1,0:T(8,128)(2,1)} %shard_map.55) | data formatting | bytes 393216

commit v5 on v4

--- a/solution.py
+++ b/solution.py
@@ -213,7 +213,7 @@
                 down_load(p, 1).wait()
             v = jnp.dot(H[...], wd[:, down_cols(p, 1)], preferred_element_type=F32)
             A[q] = v * gate
-            pl.when(q >= 1)(lambda: stage_b(q - 1))
+            stage_b(q)
             pl.when(q >= 2)(lambda: stage_c(q - 2))
 
     near = z + 1 - 2 * (z % 2)
@@ -245,7 +245,6 @@
     def pass_near(p):
         pl.when(interior)(lambda: pass_on(p, near % 2, near, z // 2, p))
 
-    stage_b(2 * pieces - 1)
     for p in range(pieces):
         if p >= pieces - 2:
             stage_c(pieces + p)

time: 72.7 us -> 67.8 us (0.933)
  Pallas kernels: 71 us -> 66.1 us
    pallas_call x1, Pallas kernels: 71 us -> 66.1 us  [fused(): pl.pallas_call(layer_kernel, out_shape=jax.ShapeDtypeStruct((rows, half),...]
where the time goes in v5:
time: 67.8 us; the launch traced here: 67.7 us
  Pallas kernels  66.1 us (97%)
  local copies, waits for them, and re-layouts  1.62 us (2%)
    pallas_call x1, Pallas kernels, fused(): pl.pallas_call(layer_kernel, out_shape=jax.ShapeDtypeStruct((rows, half),...  66.1 us
    unnamed x1, local copies, waits for them, and re-layouts  1.62 us

profile of v5, /device:TPU:0, one launch (start us, length us, event | category | flops | bytes accessed | tf_op | source)
XLA Modules:
  0.0 67.7 jit_solution(5234119807597758748)
XLA Ops:
  0.0 66.1 %shard_map.55 = bf16[64,1536]{1,0:T(8,128)(2,1)} custom-call(bf16[64,1536]{1,0:T(8,128)(2,1)} %tok.1, s32[4,64]{1,0:T(4,128)} %bitcast.2, f32[4,64]{1,0:T(4,128)} %bitcast.3, bf16[1,3072,2688]{2,1,0:T(8,128)(2,1)} %wu_hbm.1, bf16[1,2688,3072]{2,1,0:T(8,128)(2,1)} %wd_hbm.1), custom_call_target="tpu_custom_call" | custom-call | tf_op jit(solution)/shard_map/pallas_call | solution.py:298
  66.1 1.6 %copy.7 = bf16[64,1536]{1,0:T(8,128)(2,1)} copy(bf16[64,1536]{1,0:T(8,128)(2,1)} %shard_map.55) | data formatting | bytes 393216
